TPU v7x, 512 devices: a whole 4x8x8 slice. The times are simulated.
512 devices in a mesh: sector: 64 (over x, y, core), chan: 8 (over z).
Axes of the slice: x: 4, y: 8, z: 8, core: 2. Of those that a mesh axis runs over, the one named last changes fastest.
Arguments:
- surface_functions: bfloat16 [128, 256, 4096], P('sector', 'chan'), may hold values from -6 to 6, as said below
- channel_rates: float32 [128, 256], P('sector'), may hold values from 0.5 to 12
- coupling: bfloat16 [128, 256, 256], P('sector'), may hold values from -1 to 6, as said below
Outputs:
- r_inner: float32 [256, 256], P('chan', 'sector')
- r_couple: float32 [256, 256], P('chan', 'sector')
- r_outer: float32 [256, 256], P('chan', 'sector')
Inputs may be any that keep to these rules, and one draw needn't show every extreme that they name: `surface_functions`: the sum of a surface function shared by all sectors and a smaller part of each sector. `coupling`: each sector's matrix is symmetric, and each diagonal entry exceeds the sum of the magnitudes of the other entries of its row.
All inputs are finite; a program needn't handle non-finite values.
Results may differ from a plain program's by a relative error of at most 0.0003.
Values may be sent and summed in bfloat16 or wider, within the bound.
No kernel may reach another device: no remote copies, remote signals or barrier semaphores. Data moves between devices by JAX's collectives and lax.ppermute only.
A program may use at most 64 MiB of HBM per device.

v0:
```python
import jax
import jax.numpy as jnp
from jax import lax
from jax.sharding import PartitionSpec as P

G = 4096


def from_behind(array, axis, by):
    length = lax.axis_size(axis)
    pairs = [(i, i + by) for i in range(length) if 0 <= i + by < length]
    return lax.ppermute(array, axis, pairs)


def swapped(value, axis, distance):
    mask = 2**distance
    pairs = [(source, source ^ mask) for source in range(lax.axis_size(axis))]
    return lax.ppermute(value, axis, pairs)


def sector_blocks(margin_now, rates_row, coupling_row, sector_step):
    cot_term = rates_row / jnp.tanh(rates_row * sector_step)
    csc_term = rates_row / jnp.sinh(rates_row * sector_step)
    inner_block = jnp.diag(cot_term) + 0.5 * sector_step * coupling_row.astype(jnp.float32)
    half_done = jnp.dot(margin_now, inner_block, precision=lax.Precision.HIGHEST)
    block_a = jnp.dot(half_done, margin_now.T, precision=lax.Precision.HIGHEST)
    block_b = margin_now * csc_term[None, :]
    return jnp.stack([block_a, block_b, inner_block])


def merge_whole(left_part, right_part):
    factor = jnp.linalg.cholesky(left_part[2] + right_part[0])
    solved_a = jax.scipy.linalg.cho_solve((factor, True), left_part[1].T)
    solved_b = jax.scipy.linalg.cho_solve((factor, True), right_part[1])
    new_a = left_part[0] - jnp.dot(left_part[1], solved_a, precision=lax.Precision.HIGHEST)
    new_b = jnp.dot(left_part[1], solved_b, precision=lax.Precision.HIGHEST)
    new_c = right_part[2] - jnp.dot(right_part[1].T, solved_b, precision=lax.Precision.HIGHEST)
    return jnp.stack([new_a, new_b, new_c])


def per_device(surface_functions, channel_rates, coupling):
    sect_dev = surface_functions.shape[0]
    channels = channel_rates.shape[1]
    sector_count = lax.axis_size("sector")
    position = lax.axis_index("sector")
    sector_step = 1.0 / (sect_dev * sector_count)
    previous = from_behind(surface_functions[sect_dev - 1], "sector", 1)
    before = jnp.concatenate([previous[None], surface_functions[: sect_dev - 1]], axis=0)
    all_channels = lax.all_gather(surface_functions, "chan", axis=1, tiled=True)
    partial_rows = jnp.einsum(
        "sig,sjg->isj", before, all_channels, preferred_element_type=jnp.float32
    )
    margin = lax.all_gather(partial_rows, "chan", axis=0, tiled=True)
    margin = margin / G
    identity = jnp.eye(channels, dtype=jnp.float32)
    packed = None
    for sector_idx in range(sect_dev):
        margin_now = margin[:, sector_idx, :]
        if sector_idx == 0:
            margin_now = jnp.where(position == 0, identity, margin_now)
        blocks = sector_blocks(
            margin_now, channel_rates[sector_idx], coupling[sector_idx], sector_step
        )
        packed = blocks if sector_idx == 0 else merge_whole(packed, blocks)
    row_count = channels // lax.axis_size("chan")
    row_begin = lax.axis_index("chan") * row_count
    depth_count = sector_count.bit_length() - 1
    for depth_level in range(depth_count):
        partner = swapped(packed, "sector", depth_level)
        upper_half = position // 2**depth_level % 2 == 1
        left_part = jnp.where(upper_half, partner, packed)
        right_part = jnp.where(upper_half, packed, partner)
        packed = merge_whole(left_part, right_part)
    packed = lax.dynamic_slice_in_dim(packed, row_begin, row_count, 1)
    column_count = channels // sector_count
    column_begin = position * column_count
    packed = lax.dynamic_slice_in_dim(packed, column_begin, column_count, 2)
    return (packed[0], packed[1], packed[2])


def solution(mesh):
    placed = (P("sector", "chan", None), P("sector", None), P("sector", None, None))
    return jax.shard_map(
        per_device,
        mesh=mesh,
        in_specs=placed,
        out_specs=(P("chan", "sector"), P("chan", "sector"), P("chan", "sector")),
        check_vma=False,
    )
```

profile of v0, /device:TPU:30, one launch (start us, length us, event | category | flops | bytes accessed | tf_op | source)
XLA Modules:
  0.0 725.8 jit_solution(10601449324934466132)
XLA Ops:
  9.0 1.9 collective-permute-start
  12.9 3.7 collective-permute-done
  16.7 56.0 %all-gather.2.cloned.1.call-done = bf16[2,256,4096]{2,1,0:T(8,128)(2,1)} async-done(((bf16[2,32,4096]{2,1,0:T(8,128)(2,1)}), bf16[2,256,4096]{2,1,0:T(8,128)(2,1)}) %all-gather.2.cloned.1.call-update) | async-done | bytes 4194320 | tf_op jit(solution)/shard_map/all_gather | solution.py:49
  72.7 3.5 convolution_bitcast_fusion.7
  76.3 25.6 %all_gather.7 = f32[256,2,256]{2,1,0:T(2,128)S(1)} all-gather(f32[32,2,256]{2,1,0:T(2,128)S(1)} %copy.17), channel_id=1, replica_groups=mesh['sector'=64,'chan'=8] {'chan'}, dimensions={0}, use_global_device_ids=true | all-gather | bytes 589824 | tf_op jit(solution)/shard_map/all_gather | solution.py:53
  103.5 11.7 %cholesky.340 = f32[128,128]{1,0:T(8,128)S(1)} custom-call(f32[128,128]{1,0:T(8,128)S(1)} %cholesky.574), custom_call_target="Cholesky" | custom-call | tf_op jit(solution)/shard_map/jit(cholesky)/cholesky | solution.py:32
  115.3 9.8 %custom-call.32 = f32[1,128,128]{1,2,0:T(8,128)S(1)} custom-call(f32[1,128,128]{2,1,0:T(8,128)S(1)} %get-tuple-element.238), custom_call_target="InvertDiagBlocksLowerTriangular" | custom-call | tf_op jit(solution)/shard_map/jit(cholesky)/cholesky | solution.py:32
  125.6 11.7 %cholesky.357 = f32[128,128]{1,0:T(8,128)S(1)} custom-call(f32[128,128]{1,0:T(8,128)S(1)} %convolution_subtract_fusion.24), custom_call_target="Cholesky" | custom-call | tf_op jit(solution)/shard_map/jit(cholesky)/cholesky | solution.py:32
  139.6 4.3 while.28
  140.4 1.4 bitcast_dynamic-update-slice_fusion.14
  142.4 1.4 bitcast_dynamic-update-slice_fusion.14
  143.9 19.7 %custom-call.33 = f32[2,128,128]{1,2,0:T(8,128)S(1)} custom-call(f32[2,128,128]{2,1,0:T(8,128)S(1)} %get-tuple-element.91), custom_call_target="InvertDiagBlocksLowerTriangular" | custom-call | tf_op jit(solution)/shard_map/jit(_cho_solve)/triangular_solve | solution.py:33
  170.6 2.3 collective-permute-start.1
  172.9 1.8 collective-permute-done.1
  175.2 11.7 %cholesky.374 = f32[128,128]{1,0:T(8,128)S(1)} custom-call(f32[128,128]{1,0:T(8,128)S(1)} %cholesky.577), custom_call_target="Cholesky" | custom-call | tf_op jit(solution)/shard_map/jit(cholesky)/cholesky | solution.py:32
  187.0 9.8 %custom-call.35 = f32[1,128,128]{1,2,0:T(8,128)S(1)} custom-call(f32[1,128,128]{2,1,0:T(8,128)S(1)} %get-tuple-element.234), custom_call_target="InvertDiagBlocksLowerTriangular" | custom-call | tf_op jit(solution)/shard_map/jit(cholesky)/cholesky | solution.py:32
  197.3 11.7 %cholesky.391 = f32[128,128]{1,0:T(8,128)S(1)} custom-call(f32[128,128]{1,0:T(8,128)S(1)} %convolution_subtract_fusion.23), custom_call_target="Cholesky" | custom-call | tf_op jit(solution)/shard_map/jit(cholesky)/cholesky | solution.py:32
  211.8 4.3 while.29
  212.6 1.4 bitcast_dynamic-update-slice_fusion.15
  214.7 1.4 bitcast_dynamic-update-slice_fusion.15
  216.1 19.7 %custom-call.36 = f32[2,128,128]{1,2,0:T(8,128)S(1)} custom-call(f32[2,128,128]{2,1,0:T(8,128)S(1)} %get-tuple-element.93), custom_call_target="InvertDiagBlocksLowerTriangular" | custom-call | tf_op jit(solution)/shard_map/jit(_cho_solve)/triangular_solve | solution.py:33
  241.3 2.7 collective-permute-start.2
  244.0 18.8 %collective-permute-done.2 = f32[3,256,256]{1,2,0:T(8,128)S(1)} collective-permute-done((f32[3,256,256]{1,2,0:T(8,128)S(1)}, f32[3,256,256]{1,2,0:T(8,128)S(1)}, u32[]{:S(2)}, u32[]{:S(2)}) %collective-permute-start.2) | collective-permute-done | bytes 786464 | tf_op jit(solution)/shard_map/ppermute | solution.py:18
  263.3 11.7 %cholesky.408 = f32[128,128]{1,0:T(8,128)S(1)} custom-call(f32[128,128]{1,0:T(8,128)S(1)} %cholesky.580), custom_call_target="Cholesky" | custom-call | tf_op jit(solution)/shard_map/jit(cholesky)/cholesky | solution.py:32
  275.0 9.8 %custom-call.38 = f32[1,128,128]{1,2,0:T(8,128)S(1)} custom-call(f32[1,128,128]{2,1,0:T(8,128)S(1)} %get-tuple-element.230), custom_call_target="InvertDiagBlocksLowerTriangular" | custom-call | tf_op jit(solution)/shard_map/jit(cholesky)/cholesky | solution.py:32
  285.3 11.7 %cholesky.425 = f32[128,128]{1,0:T(8,128)S(1)} custom-call(f32[128,128]{1,0:T(8,128)S(1)} %convolution_subtract_fusion.22), custom_call_target="Cholesky" | custom-call | tf_op jit(solution)/shard_map/jit(cholesky)/cholesky | solution.py:32
  299.8 4.4 while.30
  300.7 1.4 bitcast_dynamic-update-slice_fusion.16
  302.8 1.4 bitcast_dynamic-update-slice_fusion.16
  304.2 19.7 %custom-call.39 = f32[2,128,128]{1,2,0:T(8,128)S(1)} custom-call(f32[2,128,128]{2,1,0:T(8,128)S(1)} %get-tuple-element.95), custom_call_target="InvertDiagBlocksLowerTriangular" | custom-call | tf_op jit(solution)/shard_map/jit(_cho_solve)/triangular_solve | solution.py:33
  329.4 2.9 collective-permute-start.3
  332.4 35.4 %collective-permute-done.3 = f32[3,256,256]{1,2,0:T(8,128)S(1)} collective-permute-done((f32[3,256,256]{1,2,0:T(8,128)S(1)}, f32[3,256,256]{1,2,0:T(8,128)S(1)}, u32[]{:S(2)}, u32[]{:S(2)}) %collective-permute-start.3) | collective-permute-done | bytes 786464 | tf_op jit(solution)/shard_map/ppermute | solution.py:18
  368.3 11.7 %cholesky.442 = f32[128,128]{1,0:T(8,128)S(1)} custom-call(f32[128,128]{1,0:T(8,128)S(1)} %cholesky.583), custom_call_target="Cholesky" | custom-call | tf_op jit(solution)/shard_map/jit(cholesky)/cholesky | solution.py:32
  380.0 9.8 %custom-call.41 = f32[1,128,128]{1,2,0:T(8,128)S(1)} custom-call(f32[1,128,128]{2,1,0:T(8,128)S(1)} %get-tuple-element.226), custom_call_target="InvertDiagBlocksLowerTriangular" | custom-call | tf_op jit(solution)/shard_map/jit(cholesky)/cholesky | solution.py:32
  390.3 11.7 %cholesky.459 = f32[128,128]{1,0:T(8,128)S(1)} custom-call(f32[128,128]{1,0:T(8,128)S(1)} %convolution_subtract_fusion.21), custom_call_target="Cholesky" | custom-call | tf_op jit(solution)/shard_map/jit(cholesky)/cholesky | solution.py:32
  404.8 4.3 while.31
  405.6 1.4 bitcast_dynamic-update-slice_fusion.17
  407.7 1.4 bitcast_dynamic-update-slice_fusion.17
  409.1 19.7 %custom-call.42 = f32[2,128,128]{1,2,0:T(8,128)S(1)} custom-call(f32[2,128,128]{2,1,0:T(8,128)S(1)} %get-tuple-element.97), custom_call_target="InvertDiagBlocksLowerTriangular" | custom-call | tf_op jit(solution)/shard_map/jit(_cho_solve)/triangular_solve | solution.py:33
  434.3 4.9 collective-permute-start.4
  439.3 35.7 %collective-permute-done.4 = f32[3,256,256]{1,2,0:T(8,128)S(1)} collective-permute-done((f32[3,256,256]{1,2,0:T(8,128)S(1)}, f32[3,256,256]{1,2,0:T(8,128)S(1)}, u32[]{:S(2)}, u32[]{:S(2)}) %collective-permute-start.4) | collective-permute-done | bytes 786464 | tf_op jit(solution)/shard_map/ppermute | solution.py:18
  475.4 11.7 %cholesky.476 = f32[128,128]{1,0:T(8,128)S(1)} custom-call(f32[128,128]{1,0:T(8,128)S(1)} %cholesky.586), custom_call_target="Cholesky" | custom-call | tf_op jit(solution)/shard_map/jit(cholesky)/cholesky | solution.py:32
  487.2 9.8 %custom-call.44 = f32[1,128,128]{1,2,0:T(8,128)S(1)} custom-call(f32[1,128,128]{2,1,0:T(8,128)S(1)} %get-tuple-element.222), custom_call_target="InvertDiagBlocksLowerTriangular" | custom-call | tf_op jit(solution)/shard_map/jit(cholesky)/cholesky | solution.py:32
  497.5 11.7 %cholesky.493 = f32[128,128]{1,0:T(8,128)S(1)} custom-call(f32[128,128]{1,0:T(8,128)S(1)} %convolution_subtract_fusion.20), custom_call_target="Cholesky" | custom-call | tf_op jit(solution)/shard_map/jit(cholesky)/cholesky | solution.py:32
  512.0 4.4 while.32
  512.9 1.4 bitcast_dynamic-update-slice_fusion.18
  514.9 1.4 bitcast_dynamic-update-slice_fusion.18
  516.4 19.7 %custom-call.45 = f32[2,128,128]{1,2,0:T(8,128)S(1)} custom-call(f32[2,128,128]{2,1,0:T(8,128)S(1)} %get-tuple-element.99), custom_call_target="InvertDiagBlocksLowerTriangular" | custom-call | tf_op jit(solution)/shard_map/jit(_cho_solve)/triangular_solve | solution.py:33
  541.6 3.3 collective-permute-start.5
  544.9 18.0 %collective-permute-done.5 = f32[3,256,256]{1,2,0:T(8,128)S(1)} collective-permute-done((f32[3,256,256]{1,2,0:T(8,128)S(1)}, f32[3,256,256]{1,2,0:T(8,128)S(1)}, u32[]{:S(2)}, u32[]{:S(2)}) %collective-permute-start.5) | collective-permute-done | bytes 786464 | tf_op jit(solution)/shard_map/ppermute | solution.py:18
  563.4 11.7 %cholesky.510 = f32[128,128]{1,0:T(8,128)S(1)} custom-call(f32[128,128]{1,0:T(8,128)S(1)} %cholesky.589), custom_call_target="Cholesky" | custom-call | tf_op jit(solution)/shard_map/jit(cholesky)/cholesky | solution.py:32
  575.2 9.8 %custom-call.47 = f32[1,128,128]{1,2,0:T(8,128)S(1)} custom-call(f32[1,128,128]{2,1,0:T(8,128)S(1)} %get-tuple-element.218), custom_call_target="InvertDiagBlocksLowerTriangular" | custom-call | tf_op jit(solution)/shard_map/jit(cholesky)/cholesky | solution.py:32
  585.5 11.7 %cholesky.527 = f32[128,128]{1,0:T(8,128)S(1)} custom-call(f32[128,128]{1,0:T(8,128)S(1)} %convolution_subtract_fusion.19), custom_call_target="Cholesky" | custom-call | tf_op jit(solution)/shard_map/jit(cholesky)/cholesky | solution.py:32
  600.0 4.3 while.33
  600.8 1.4 bitcast_dynamic-update-slice_fusion.19
  602.8 1.4 bitcast_dynamic-update-slice_fusion.19
  604.3 19.7 %custom-call.48 = f32[2,128,128]{1,2,0:T(8,128)S(1)} custom-call(f32[2,128,128]{2,1,0:T(8,128)S(1)} %get-tuple-element.101), custom_call_target="InvertDiagBlocksLowerTriangular" | custom-call | tf_op jit(solution)/shard_map/jit(_cho_solve)/triangular_solve | solution.py:33
  629.5 3.6 collective-permute-start.6
  633.1 18.3 %collective-permute-done.6 = f32[3,256,256]{1,2,0:T(8,128)S(1)} collective-permute-done((f32[3,256,256]{1,2,0:T(8,128)S(1)}, f32[3,256,256]{1,2,0:T(8,128)S(1)}, u32[]{:S(2)}, u32[]{:S(2)}) %collective-permute-start.6) | collective-permute-done | bytes 786464 | tf_op jit(solution)/shard_map/ppermute | solution.py:18
  652.0 11.7 %cholesky.544 = f32[128,128]{1,0:T(8,128)S(1)} custom-call(f32[128,128]{1,0:T(8,128)S(1)} %cholesky.592), custom_call_target="Cholesky" | custom-call | tf_op jit(solution)/shard_map/jit(cholesky)/cholesky | solution.py:32
  663.7 9.8 %custom-call.50 = f32[1,128,128]{1,2,0:T(8,128)S(1)} custom-call(f32[1,128,128]{2,1,0:T(8,128)S(1)} %get-tuple-element.214), custom_call_target="InvertDiagBlocksLowerTriangular" | custom-call | tf_op jit(solution)/shard_map/jit(cholesky)/cholesky | solution.py:32
  674.0 11.7 %cholesky.561 = f32[128,128]{1,0:T(8,128)S(1)} custom-call(f32[128,128]{1,0:T(8,128)S(1)} %convolution_subtract_fusion.18), custom_call_target="Cholesky" | custom-call | tf_op jit(solution)/shard_map/jit(cholesky)/cholesky | solution.py:32
  688.4 4.3 while.34
  692.7 19.7 %custom-call.51 = f32[2,128,128]{1,2,0:T(8,128)S(1)} custom-call(f32[2,128,128]{2,1,0:T(8,128)S(1)} %get-tuple-element.103), custom_call_target="InvertDiagBlocksLowerTriangular" | custom-call | tf_op jit(solution)/shard_map/jit(_cho_solve)/triangular_solve | solution.py:33
  (257 shorter events, 72.2 us)
Async XLA Ops:
  7.2 65.5 %all-gather.2.cloned.1.call-start = ((), (), s32[]{:S(2)}) async-start(), calls=%async_computation | async-start | bytes 4718592 | tf_op jit(solution)/shard_map/all_gather | solution.py:49
  9.0 7.7 %collective-permute-start = (bf16[32,4096]{1,0:T(8,128)(2,1)S(1)}, bf16[32,4096]{1,0:T(8,128)(2,1)S(1)}, u32[]{:S(2)}, u32[]{:S(2)}) collective-permute-start(bf16[32,4096]{1,0:T(8,128)(2,1)S(1)} %get-tuple-element.207), channel_id=1, source_target_pairs={{0,8},{8,16},{16,24},{24,32},{32,40},{40,48},{48,56},{56,64},{64,7... | collective-permute-start | bytes 786440 | tf_op jit(solution)/shard_map/ppermute | solution.py:12
  170.6 4.2 collective-permute-start.1
  241.3 21.5 %collective-permute-start.2 = (f32[3,256,256]{1,2,0:T(8,128)S(1)}, f32[3,256,256]{1,2,0:T(8,128)S(1)}, u32[]{:S(2)}, u32[]{:S(2)}) collective-permute-start(f32[3,256,256]{1,2,0:T(8,128)S(1)} %pad_maximum_fusion.1), channel_id=1, source_target_pairs={{0,16},{8,24},{16,0},{24,8},{32,48},{40,56},{48,32},{56,40},{64,80... | collective-permute-start | bytes 2359304 | tf_op jit(solution)/shard_map/ppermute | solution.py:18
  329.4 38.4 %collective-permute-start.3 = (f32[3,256,256]{1,2,0:T(8,128)S(1)}, f32[3,256,256]{1,2,0:T(8,128)S(1)}, u32[]{:S(2)}, u32[]{:S(2)}) collective-permute-start(f32[3,256,256]{1,2,0:T(8,128)S(1)} %pad_maximum_fusion.2), channel_id=1, source_target_pairs={{0,32},{8,40},{16,48},{24,56},{32,0},{40,8},{48,16},{56,24},{64,96... | collective-permute-start | bytes 2359304 | tf_op jit(solution)/shard_map/ppermute | solution.py:18
  434.3 40.6 %collective-permute-start.4 = (f32[3,256,256]{1,2,0:T(8,128)S(1)}, f32[3,256,256]{1,2,0:T(8,128)S(1)}, u32[]{:S(2)}, u32[]{:S(2)}) collective-permute-start(f32[3,256,256]{1,2,0:T(8,128)S(1)} %pad_maximum_fusion.3), channel_id=1, source_target_pairs={{0,64},{8,72},{16,80},{24,88},{32,96},{40,104},{48,112},{56,120},{... | collective-permute-start | bytes 2359304 | tf_op jit(solution)/shard_map/ppermute | solution.py:18
  541.6 21.4 %collective-permute-start.5 = (f32[3,256,256]{1,2,0:T(8,128)S(1)}, f32[3,256,256]{1,2,0:T(8,128)S(1)}, u32[]{:S(2)}, u32[]{:S(2)}) collective-permute-start(f32[3,256,256]{1,2,0:T(8,128)S(1)} %pad_maximum_fusion.4), channel_id=1, source_target_pairs={{0,128},{8,136},{16,144},{24,152},{32,160},{40,168},{48,176},{56,1... | collective-permute-start | bytes 2359304 | tf_op jit(solution)/shard_map/ppermute | solution.py:18
  629.5 22.0 %collective-permute-start.6 = (f32[3,256,256]{1,2,0:T(8,128)S(1)}, f32[3,256,256]{1,2,0:T(8,128)S(1)}, u32[]{:S(2)}, u32[]{:S(2)}) collective-permute-start(f32[3,256,256]{1,2,0:T(8,128)S(1)} %pad_maximum_fusion.5), channel_id=1, source_target_pairs={{0,256},{8,264},{16,272},{24,280},{32,288},{40,296},{48,304},{56,3... | collective-permute-start | bytes 2359304 | tf_op jit(solution)/shard_map/ppermute | solution.py:18
Sparse Core Ops, SparseCore 0:
  10.1 62.5 all-gather.1
where the time goes:
time: 736 us; the launch traced here: 726 us
  other arithmetic  383 us (52%)
  waiting for transfers between devices  189 us (26%)
  matrix products  46.8 us (6%)
  local copies, waits for them, and re-layouts  32.6 us (4%)
  between operations  25.7 us (3%)
  blocking collectives  25.6 us (3%)
  starting transfers between devices  21.6 us (3%)
    another operation x48, other arithmetic, merge_whole(): factor = jnp.linalg.cholesky(left_part[2] + right_part[0])  242 us
    another operation x15, other arithmetic, merge_whole(): solved_a = jax.scipy.linalg.cho_solve((factor, True), left_part[1].T)  138 us
    ppermute x6, waiting for transfers between devices, swapped(): return lax.ppermute(value, axis, pairs)  128 us
    all_gather x1, waiting for transfers between devices, per_device(): all_channels = lax.all_gather(surface_functions, 'chan', axis=1, tiled=True)  56 us
    another operation x50, local copies, waits for them, and re-layouts, merge_whole(): solved_a = jax.scipy.linalg.cho_solve((factor, True), left_part[1].T)  28.4 us
    all_gather x1, blocking collectives, per_device(): margin = lax.all_gather(partial_rows, 'chan', axis=0, tiled=True)  25.6 us
    ppermute x6, starting transfers between devices, swapped(): return lax.ppermute(value, axis, pairs)  19.6 us
  transfers between devices with their start and end apart: 8, of which 8 were waited for; matrix products, arithmetic and copies ran while one was open for 0% of the time, Pallas kernels for 0%

commit v1 on v0

v1 whole, which is shorter than its diff:
```python
import functools

import jax
import jax.numpy as jnp
from jax import lax
from jax.experimental import pallas as pl
from jax.experimental.pallas import tpu as pltpu
from jax.sharding import PartitionSpec as P

F32 = jnp.float32
BF16 = jnp.bfloat16
NN = (((1,), (0,)), ((), ()))
NT = (((1,), (1,)), ((), ()))
TN = (((0,), (0,)), ((), ()))
SQUARINGS = 7
TOLERANCE = 1e-5
PARAMS = pltpu.CompilerParams(vmem_limit_bytes=32 * 2**20)
VMEM = pl.BlockSpec(memory_space=pltpu.VMEM)
SMEM = pl.BlockSpec(memory_space=pltpu.SMEM)


def parts(x):
    high = x.astype(BF16)
    rest = x - high.astype(F32)
    middle = rest.astype(BF16)
    return high, middle, (rest - middle.astype(F32)).astype(BF16)


def dot1(a, b, dims=NN):
    return lax.dot_general(a, b, dims, preferred_element_type=F32)


def dot3(a, b, dims=NN):
    return dot1(a[0], b[0], dims) + (dot1(a[0], b[1], dims) + dot1(a[1], b[0], dims))


def dot6(a, b, dims=NN):
    low = dot1(a[0], b[2], dims) + dot1(a[1], b[1], dims) + dot1(a[2], b[0], dims)
    return dot1(a[0], b[0], dims) + ((dot1(a[0], b[1], dims) + dot1(a[1], b[0], dims)) + low)


def grid_of(n):
    return (
        lax.broadcasted_iota(jnp.int32, (n, n), 0),
        lax.broadcasted_iota(jnp.int32, (n, n), 1),
    )


def unit(n):
    row, column = grid_of(n)
    return jnp.where(row == column, F32(1), F32(0))


def invert(d_ref, x_ref):
    n = d_ref.shape[0]
    d = d_ref[...]
    bound = jnp.max(jnp.sum(jnp.abs(d), axis=0, keepdims=True), axis=1, keepdims=True)
    alpha = 1.9 / bound
    e = unit(n) - alpha * d
    x = unit(n) + e
    for _ in range(SQUARINGS):
        rounded = e.astype(BF16)
        e = dot1(rounded, rounded)
        x = x + dot1(x.astype(BF16), e.astype(BF16))
    x_ref[...] = alpha * x
    split = parts(d_ref[...])

    def going(state):
        return jnp.logical_and(state[0] < 8, jnp.logical_not(state[1] < TOLERANCE))

    def refine(state):
        x_parts = parts(x_ref[...])
        residual = unit(n) - dot6(split, x_parts)
        x_ref[...] = x_ref[...] + dot3(x_parts, parts(residual))
        return state[0] + 1, jnp.sum(residual * residual)

    _, left = lax.while_loop(going, refine, (0, F32(1)))

    @pl.when(jnp.logical_not(left < TOLERANCE))
    def _():
        x_ref[...] = alpha * unit(n)

        def still(state):
            return jnp.logical_and(state[0] < 60, jnp.logical_not(state[1] < TOLERANCE**2))

        def careful(state):
            before = x_ref[...]
            residual = unit(n) - jnp.dot(d_ref[...], before, precision=lax.Precision.HIGHEST)
            x_ref[...] = before + jnp.dot(before, residual, precision=lax.Precision.HIGHEST)
            return state[0] + 1, jnp.sum(residual * residual)

        lax.while_loop(still, careful, (0, F32(1)))


def combine(left, right, x_ref, out_ref):
    b1, b2, x = parts(left(1)), parts(right(1)), parts(x_ref[...])
    w1, w2 = parts(dot6(b1, x)), parts(dot6(x, b2))
    new_a = left(0) - dot6(w1, b1, NT)
    new_b = dot6(w1, b2)
    new_c = right(2) - dot6(b2, w2, TN)
    out_ref[0] = new_a
    out_ref[1] = new_b
    out_ref[2] = new_c


def pack(core, out_ref, send_ref):
    n = out_ref.shape[-1]
    row, column = grid_of(n)
    last = out_ref[2]
    both = jnp.where(row >= column, out_ref[0], last)
    send_ref[0:n] = jnp.where(core == 0, both, out_ref[1])
    diagonal = jnp.sum(jnp.where(row == column, last, F32(0)), axis=0, keepdims=True)
    send_ref[n : n + 8] = jnp.broadcast_to(diagonal, (8, n))


def leaf_kernel(flags_ref, margin_ref, cot_ref, csc_ref, coupling_ref, out_ref, d_ref, x_ref, a_ref, b_ref, c_ref):
    n = d_ref.shape[0]
    row, column = grid_of(n)
    half_step = 0.5 / (2 * flags_ref[1]).astype(F32)

    def sector(s):
        margin = margin_ref[:, s].reshape(n, n)
        if s == 0:
            margin = jnp.where(flags_ref[0] == 0, unit(n), margin)
        inner = jnp.where(row == column, cot_ref[s : s + 1, :], F32(0)) + half_step * coupling_ref[s].astype(F32)
        m = parts(margin)
        a_ref[s] = dot6(parts(dot6(m, parts(inner))), m, NT)
        b_ref[s] = margin * csc_ref[s : s + 1, :]
        c_ref[s] = inner

    sector(1)
    sector(0)
    d_ref[...] = c_ref[0] + a_ref[1]
    invert(d_ref, x_ref)
    blocks = (a_ref, b_ref, c_ref)
    combine(lambda i: blocks[i][0], lambda i: blocks[i][1], x_ref, out_ref)


def leaf(flags, margin, cot, csc, coupling):
    n = coupling.shape[-1]
    return pl.pallas_call(
        leaf_kernel,
        out_shape=jax.ShapeDtypeStruct((3, n, n), F32),
        in_specs=[SMEM, VMEM, VMEM, VMEM, VMEM],
        out_specs=VMEM,
        scratch_shapes=[pltpu.VMEM((n, n), F32)] * 2 + [pltpu.VMEM((2, n, n), F32)] * 3,
        compiler_params=PARAMS,
        name="leaf",
    )(flags, margin, cot, csc, coupling)


def merge_refs(upper, own_ref, other_ref, out_ref, d_ref, x_ref):
    d_ref[...] = jnp.where(upper, other_ref[2] + own_ref[0], own_ref[2] + other_ref[0])
    invert(d_ref, x_ref)
    combine(
        lambda i: jnp.where(upper, other_ref[i], own_ref[i]),
        lambda i: jnp.where(upper, own_ref[i], other_ref[i]),
        x_ref,
        out_ref,
    )


def core_kernel(flags_ref, own_ref, other_ref, out_ref, send_ref, d_ref, x_ref):
    core = flags_ref[2]
    merge_refs(core == 1, own_ref, other_ref, out_ref, d_ref, x_ref)
    pack(core, out_ref, send_ref)


def core_merge(flags, own, other):
    n = own.shape[-1]
    return pl.pallas_call(
        core_kernel,
        out_shape=(jax.ShapeDtypeStruct((3, n, n), F32), jax.ShapeDtypeStruct((n + 8, n), F32)),
        in_specs=[SMEM, VMEM, VMEM],
        out_specs=(VMEM, VMEM),
        scratch_shapes=[pltpu.VMEM((n, n), F32)] * 2,
        compiler_params=PARAMS,
        name="core_merge",
    )(flags, own, other)


def chip_kernel(level, flags_ref, own_ref, came_ref, swapped_ref, out_ref, send_ref, d_ref, x_ref, other_ref):
    n = d_ref.shape[0]
    core = flags_ref[2]
    active = flags_ref[4 + 2 * level] == 1

    @pl.when(active)
    def _():
        row, column = grid_of(n)
        both = jnp.where(core == 0, came_ref[0:n], swapped_ref[0:n])
        diagonal = jnp.where(core == 0, came_ref[n : n + 1], swapped_ref[n : n + 1])
        turned = both.T
        other_ref[0] = jnp.where(row >= column, both, turned)
        other_ref[1] = jnp.where(core == 0, swapped_ref[0:n], came_ref[0:n])
        other_ref[2] = jnp.where(row == column, diagonal, jnp.where(row < column, both, turned))
        merge_refs(flags_ref[5 + 2 * level] == 1, own_ref, other_ref, out_ref, d_ref, x_ref)
        pack(core, out_ref, send_ref)

    @pl.when(jnp.logical_not(active))
    def _():
        out_ref[...] = own_ref[...]
        send_ref[...] = jnp.zeros_like(send_ref)


def chip_merge(level, flags, own, came, swapped):
    n = own.shape[-1]
    return pl.pallas_call(
        functools.partial(chip_kernel, level),
        out_shape=(jax.ShapeDtypeStruct((3, n, n), F32), jax.ShapeDtypeStruct((n + 8, n), F32)),
        in_specs=[SMEM, VMEM, VMEM, VMEM],
        out_specs=(VMEM, VMEM),
        scratch_shapes=[pltpu.VMEM((n, n), F32)] * 2 + [pltpu.VMEM((3, n, n), F32)],
        compiler_params=PARAMS,
        name="chip_merge",
    )(flags, own, came, swapped)


def margin_kernel(own_ref, before_ref, out_ref):
    shards, _, rows, depth = own_ref.shape
    n = shards * rows
    first = own_ref[:, 0].reshape(n, depth)
    second = own_ref[:, 1].reshape(n, depth)
    out_ref[:, 1] = dot1(first, second, NT).reshape(shards, rows, n)
    out_ref[:, 0] = dot1(before_ref[...].reshape(n, depth), first, NT).reshape(shards, rows, n)


def margin_parts(own, before):
    shards, sectors, rows, _ = own.shape
    return pl.pallas_call(
        margin_kernel,
        out_shape=jax.ShapeDtypeStruct((shards, sectors, rows, shards * rows), F32),
        in_specs=[VMEM, VMEM],
        out_specs=VMEM,
        compiler_params=PARAMS,
        name="margin_parts",
    )(own, before)


def exchange(array):
    return lax.all_to_all(array, "chan", split_axis=0, concat_axis=0, tiled=True)


YS = 8
ENDS = (0, 3, 4, 7)


def place(position):
    return position // (2 * YS), position // 2 % YS, position % 2


def spot(x, y, core):
    return (x * YS + y) * 2 + core


def levels(xs):
    result = [
        (lambda x, y: (x, y ^ 1), range(YS), ("y", 0)),
        (lambda x, y: (x, y ^ 2), ENDS, ("y", 1)),
        (lambda x, y: (x, YS - 1 - y), ENDS, ("y", 2)),
    ]
    for bit in range(xs.bit_length() - 1):
        mask = 2 ** (bit + 1) - 1
        result.append((lambda x, y, mask=mask: (x ^ mask, y), ENDS, ("x", bit)))
    return result


def per_device(surface_functions, channel_rates, coupling):
    sectors, rows, points = surface_functions.shape
    n = channel_rates.shape[1]
    shards = lax.axis_size("chan")
    count = lax.axis_size("sector")
    position = lax.axis_index("sector")
    plan = levels(count // (2 * YS))
    x, y, core = place(position)
    at_end = (y == ENDS[0]) | (y == ENDS[1]) | (y == ENDS[2]) | (y == ENDS[3])
    words = [position, jnp.int32(count), core, jnp.int32(0)]
    for _, takers, (axis, bit) in plan:
        words.append(jnp.int32(1) if len(takers) == YS else at_end.astype(jnp.int32))
        words.append((x if axis == "x" else y) >> bit & 1)
    flags = jnp.stack([jnp.asarray(word, jnp.int32) for word in words])

    step = 1.0 / (sectors * count)
    cot = channel_rates / jnp.tanh(channel_rates * step)
    csc = channel_rates / jnp.sinh(channel_rates * step)

    cut = surface_functions.reshape(sectors, rows, shards, points // shards)
    own = exchange(jnp.transpose(cut, (2, 0, 1, 3)))
    before = lax.ppermute(own[:, sectors - 1], "sector", [(i, i + 1) for i in range(count - 1)])
    partial = exchange(margin_parts(own, before))
    summed = jnp.sum(partial, axis=0) / points
    margin = exchange(jnp.broadcast_to(summed[None], (shards, sectors, rows, n)))

    packed = leaf(flags, margin, cot, csc, coupling)
    cores = [(i, i ^ 1) for i in range(count)]
    packed, send = core_merge(flags, packed, lax.ppermute(packed, "sector", cores))
    for level, (partner, takers, _) in enumerate(plan):
        pairs = []
        for i in range(count):
            xi, yi, ci = place(i)
            if yi in takers:
                pairs.append((spot(*partner(xi, yi), ci), i))
        came = lax.ppermute(send, "sector", pairs)
        swapped = lax.ppermute(came, "sector", cores)
        packed, send = chip_merge(level, flags, packed, came, swapped)

    wide = n // count
    mine = lax.dynamic_slice_in_dim(packed, lax.axis_index("chan") * rows, rows, 1)
    next_door = spot(x, y ^ 1, core)
    for_next = lax.dynamic_slice_in_dim(mine, next_door * wide, wide, 2)
    pairs = []
    for i in range(count):
        xi, yi, ci = place(i)
        if yi not in ENDS:
            pairs.append((spot(xi, yi ^ 1, ci), i))
    brought = lax.ppermute(for_next, "sector", pairs)
    result = jnp.where(at_end, lax.dynamic_slice_in_dim(mine, position * wide, wide, 2), brought)
    return (result[0], result[1], result[2])


def solution(mesh):
    placed = (P("sector", "chan", None), P("sector", None), P("sector", None, None))
    return jax.shard_map(
        per_device,
        mesh=mesh,
        in_specs=placed,
        out_specs=(P("chan", "sector"), P("chan", "sector"), P("chan", "sector")),
        check_vma=False,
    )
```

time: 736 us -> 208 us (0.28)
  the two profiles are of different devices: /device:TPU:30 before, /device:TPU:16 now
where the time goes in v1:
time: 208 us
  waiting for transfers between devices  104 us (50%)
  blocking collectives  47.2 us (23%)
  starting transfers between devices  29.2 us (14%)
  Pallas kernels  21.2 us (10%)
  local copies, waits for them, and re-layouts  5.01 us (2%)
    ppermute x1, waiting for transfers between devices, per_device(): brought = lax.ppermute(for_next, 'sector', pairs)  60.9 us
    all_to_all x2, blocking collectives, exchange(): lax.all_to_all(array, 'chan', split_axis=0, concat_axis=0, tiled=True)  47.2 us
    all_to_all x1, waiting for transfers between devices, exchange(): lax.all_to_all(array, 'chan', split_axis=0, concat_axis=0, tiled=True)  14.7 us
    ppermute x5, waiting for transfers between devices, per_device(): came = lax.ppermute(send, 'sector', pairs)  13 us
    ppermute x5, starting transfers between devices, per_device(): came = lax.ppermute(send, 'sector', pairs)  10.5 us
    ppermute x5, starting transfers between devices, per_device(): swapped = lax.ppermute(came, 'sector', cores)  9.95 us
    pallas_call x5, Pallas kernels, chip_merge(): pl.pallas_call(functools.partial(chip_kernel, level), out_shape=(jax.Shap...  9.1 us
    ppermute x5, waiting for transfers between devices, per_device(): swapped = lax.ppermute(came, 'sector', cores)  7.16 us
  transfers between devices with their start and end apart: 14, of which 11 were waited for; matrix products, arithmetic and copies ran while one was open for 0% of the time, Pallas kernels for 0%

profile of v1, /device:TPU:16, one launch (start us, length us, event | category | flops | bytes accessed | tf_op | source)
XLA Modules:
  0.0 207.5 jit_solution(7515433424778292476)
XLA Ops:
  0.6 1.2 copy.21
  1.9 0.2 copy.15
  2.1 27.6 %all_to_all.15.own_ref = bf16[8,2,32,512]{3,2,1,0:T(8,128)(2,1)S(1)} all-to-all(bf16[8,2,32,512]{3,2,1,0:T(8,128)(2,1)S(1)} %copy.15), channel_id=1, replica_groups=mesh['sector'=64,'chan'=8] {'chan'}, dimensions={0} | all-to-all | bytes 1048576 | tf_op jit(solution)/shard_map/all_to_all | solution.py:240
  29.7 1.9 collective-permute-start
  31.6 5.8 %collective-permute-done.before_ref = bf16[8,32,512]{2,1,0:T(8,128)(2,1)S(1)} collective-permute-done((bf16[8,32,512]{2,1,0:T(8,128)(2,1)S(1)}, bf16[8,32,512]{2,1,0:T(8,128)(2,1)S(1)}, u32[]{:S(2)}, u32[]{:S(2)}) %collective-permute-start) | collective-permute-done | bytes 262176 | tf_op jit(solution)/shard_map/ppermute | solution.py:288
  37.4 0.3 margin_parts.1
  37.7 19.6 %all_to_all.16 = f32[8,2,32,256]{3,2,1,0:T(8,128)S(1)} all-to-all(f32[8,2,32,256]{3,2,1,0:T(8,128)S(1)} %margin_parts.1), channel_id=1, replica_groups=mesh['sector'=64,'chan'=8] {'chan'}, dimensions={0} | all-to-all | bytes 1048576 | tf_op jit(solution)/shard_map/all_to_all | solution.py:240
  57.3 0.9 broadcast_in_dim.2
  58.2 0.0 copy-start
  58.2 3.6 %all-to-all-start.2 = ((f32[8,2,32,256]{3,2,1,0:T(8,128)}), f32[8,2,32,256]{3,2,1,0:T(8,128)S(1)}, u32[]{:S(2)}, u32[]{:S(2)}) async-start(f32[8,2,32,256]{3,2,1,0:T(8,128)} %broadcast_in_dim.2), calls=%async_computation.2 | async-start | bytes 1048576 | tf_op jit(solution)/shard_map/all_to_all | solution.py:240
  61.9 0.0 copy-start.1
  61.9 0.1 stack.42.flags_ref
  62.0 0.6 copy-done.1
  62.6 14.7 %all-to-all-done.2.margin_ref = f32[8,2,32,256]{3,2,1,0:T(8,128)S(1)} async-done(((f32[8,2,32,256]{3,2,1,0:T(8,128)}), f32[8,2,32,256]{3,2,1,0:T(8,128)S(1)}, u32[]{:S(2)}, u32[]{:S(2)}) %all-to-all-start.2) | async-done | bytes 524320 | tf_op jit(solution)/shard_map/all_to_all | solution.py:240
  77.3 0.0 copy-done
  77.3 6.3 %leaf.1.own_ref = f32[3,256,256]{2,1,0:T(8,128)S(1)} custom-call(s32[14]{0:T(128)S(1)} %stack.42.flags_ref, f32[8,2,32,256]{3,2,1,0:T(8,128)S(1)} %all-to-all-done.2.margin_ref, f32[2,256]{1,0:T(2,128)S(1)} %get-tuple-element.29.cot_ref, f32[2,256]{1,0:T(2,128)S(1)} %get-tuple-element.28.csc_ref, bf16[2,256,256]{2,1,0:T(8,128)(2,1)S(1)} %copy-done), custom_call_target="tpu_custom_call" | custom-call | tf_op jit(solution)/shard_map/leaf/pallas_call | solution.py:141
  83.6 1.9 collective-permute-start.1
  85.6 2.3 %collective-permute-done.1.other_ref = f32[3,256,256]{2,1,0:T(8,128)S(1)} collective-permute-done((f32[3,256,256]{2,1,0:T(8,128)S(1)}, f32[3,256,256]{2,1,0:T(8,128)S(1)}, u32[]{:S(2)}, u32[]{:S(2)}) %collective-permute-start.1) | collective-permute-done | bytes 786464 | tf_op jit(solution)/shard_map/ppermute | solution.py:295
  87.8 5.4 %core_merge.1 = (f32[3,256,256]{2,1,0:T(8,128)S(1)}, f32[264,256]{1,0:T(8,128)S(1)}) custom-call(s32[14]{0:T(128)S(1)} %stack.42.flags_ref, f32[3,256,256]{2,1,0:T(8,128)S(1)} %leaf.1.own_ref, f32[3,256,256]{2,1,0:T(8,128)S(1)} %collective-permute-done.1.other_ref), custom_call_target="tpu_custom_call" | custom-call | tf_op jit(solution)/shard_map/core_merge/pallas_call | solution.py:171
  93.2 7.2 %collective-permute-start.2 = (f32[264,256]{1,0:T(8,128)S(1)}, f32[264,256]{1,0:T(8,128)S(1)}, u32[]{:S(2)}, u32[]{:S(2)}) collective-permute-start(f32[264,256]{1,0:T(8,128)S(1)} %get-tuple-element.15), channel_id=1, source_target_pairs={{16,0},{24,8},{0,16},{8,24},{48,32},{56,40},{32,48},{40,56},{80,64... | collective-permute-start | bytes 811016 | tf_op jit(solution)/shard_map/ppermute | solution.py:302
  100.4 6.8 %collective-permute-done.2.came_ref = f32[264,256]{1,0:T(8,128)S(1)} collective-permute-done((f32[264,256]{1,0:T(8,128)S(1)}, f32[264,256]{1,0:T(8,128)S(1)}, u32[]{:S(2)}, u32[]{:S(2)}) %collective-permute-start.2) | collective-permute-done | bytes 270368 | tf_op jit(solution)/shard_map/ppermute | solution.py:302
  107.1 1.9 collective-permute-start.3
  109.1 1.5 collective-permute-done.3.swapped_ref
  110.6 5.7 %chip_merge.5 = (f32[3,256,256]{2,1,0:T(8,128)S(1)}, f32[264,256]{1,0:T(8,128)S(1)}) custom-call(s32[14]{0:T(128)S(1)} %stack.42.flags_ref, f32[3,256,256]{2,1,0:T(8,128)S(1)} %get-tuple-element.14.own_ref, f32[264,256]{1,0:T(8,128)S(1)} %collective-permute-done.2.came_ref, f32[264,256]{1,0:T(8,128)S(1)} %collective-permute-done.3.swapped_ref), custom_call_target="tpu_custom_call" | custom-call | tf_op jit(solution)/shard_map/chip_merge/pallas_call | solution.py:207
  116.3 1.3 collective-permute-start.4
  117.6 6.3 %collective-permute-done.4.came_ref = f32[264,256]{1,0:T(8,128)S(1)} collective-permute-done((f32[264,256]{1,0:T(8,128)S(1)}, f32[264,256]{1,0:T(8,128)S(1)}, u32[]{:S(2)}, u32[]{:S(2)}) %collective-permute-start.4) | collective-permute-done | bytes 270368 | tf_op jit(solution)/shard_map/ppermute | solution.py:302
  123.8 1.9 collective-permute-start.5
  125.8 1.5 collective-permute-done.5.swapped_ref
  127.3 0.6 chip_merge.6
  127.9 0.7 collective-permute-start.6
  128.6 0.0 collective-permute-done.6.came_ref
  128.6 2.0 collective-permute-start.7
  130.6 1.4 collective-permute-done.7.swapped_ref
  132.0 0.6 chip_merge.7
  132.7 0.7 collective-permute-start.8
  133.3 0.0 collective-permute-done.8.came_ref
  133.4 2.0 collective-permute-start.9
  135.4 1.4 collective-permute-done.9.swapped_ref
  136.8 0.6 chip_merge.8
  137.4 0.7 collective-permute-start.10
  138.1 0.0 collective-permute-done.10.came_ref
  138.1 2.0 collective-permute-start.11
  140.2 1.4 collective-permute-done.11.swapped_ref
  141.6 1.6 chip_merge.9
  143.1 0.1 constant_dynamic-slice_fusion
  143.2 1.3 collective-permute-start.12
  144.5 60.9 %collective-permute-done.12 = f32[3,32,4]{2,1,0:T(8,128)S(1)} collective-permute-done((f32[3,32,4]{2,1,0:T(8,128)S(1)}, f32[3,32,4]{2,1,0:T(8,128)S(1)}, u32[]{:S(2)}, u32[]{:S(2)}) %collective-permute-start.12) | collective-permute-done | bytes 1568 | tf_op jit(solution)/shard_map/ppermute | solution.py:315
  205.5 0.1 dynamic-slice_select_fusion
  205.6 0.7 copy.19
  206.2 0.7 copy.18
  206.9 0.7 copy.17
  (6 shorter events, 0.1 us)
Async XLA Ops:
  29.7 7.7 %collective-permute-start = (bf16[8,32,512]{2,1,0:T(8,128)(2,1)S(1)}, bf16[8,32,512]{2,1,0:T(8,128)(2,1)S(1)}, u32[]{:S(2)}, u32[]{:S(2)}) collective-permute-start(bf16[8,32,512]{2,1,0:T(8,128)(2,1)S(1)} %slice_bitcast_fusion), channel_id=1, source_target_pairs={{0,8},{8,16},{16,24},{24,32},{32,40},{40,48},{48,56},{56,64},{64,7... | collective-permute-start | bytes 786440 | tf_op jit(solution)/shard_map/ppermute | solution.py:288
  58.2 19.1 %copy-start = (bf16[2,256,256]{2,1,0:T(8,128)(2,1)S(1)}, bf16[2,256,256]{2,1,0:T(8,128)(2,1)}, u32[]{:S(2)}) copy-start(bf16[2,256,256]{2,1,0:T(8,128)(2,1)} %coupling_ref.1) | copy-start | bytes 786436
  58.2 19.1 %all-to-all-start.2 = ((f32[8,2,32,256]{3,2,1,0:T(8,128)}), f32[8,2,32,256]{3,2,1,0:T(8,128)S(1)}, u32[]{:S(2)}, u32[]{:S(2)}) async-start(f32[8,2,32,256]{3,2,1,0:T(8,128)} %broadcast_in_dim.2), calls=%async_computation.2 | async-start | bytes 1048576 | tf_op jit(solution)/shard_map/all_to_all | solution.py:240
  61.9 0.7 copy-start.1
  83.6 4.2 %collective-permute-start.1 = (f32[3,256,256]{2,1,0:T(8,128)S(1)}, f32[3,256,256]{2,1,0:T(8,128)S(1)}, u32[]{:S(2)}, u32[]{:S(2)}) collective-permute-start(f32[3,256,256]{2,1,0:T(8,128)S(1)} %leaf.1.own_ref), channel_id=1, source_target_pairs={{0,8},{8,0},{16,24},{24,16},{32,40},{40,32},{48,56},{56,48},{64,72... | collective-permute-start | bytes 2359304 | tf_op jit(solution)/shard_map/ppermute | solution.py:295
  93.2 13.9 %collective-permute-start.2 = (f32[264,256]{1,0:T(8,128)S(1)}, f32[264,256]{1,0:T(8,128)S(1)}, u32[]{:S(2)}, u32[]{:S(2)}) collective-permute-start(f32[264,256]{1,0:T(8,128)S(1)} %get-tuple-element.15), channel_id=1, source_target_pairs={{16,0},{24,8},{0,16},{8,24},{48,32},{56,40},{32,48},{40,56},{80,64... | collective-permute-start | bytes 811016 | tf_op jit(solution)/shard_map/ppermute | solution.py:302
  107.1 3.4 %collective-permute-start.3 = (f32[264,256]{1,0:T(8,128)S(1)}, f32[264,256]{1,0:T(8,128)S(1)}, u32[]{:S(2)}, u32[]{:S(2)}) collective-permute-start(f32[264,256]{1,0:T(8,128)S(1)} %collective-permute-done.2.came_ref), channel_id=1, source_target_pairs={{0,8},{8,0},{16,24},{24,16},{32,40},{40,32},{48,56},{56,48},{64,72... | collective-permute-start | bytes 811016 | tf_op jit(solution)/shard_map/ppermute | solution.py:303
  116.3 7.6 %collective-permute-start.4 = (f32[264,256]{1,0:T(8,128)S(1)}, f32[264,256]{1,0:T(8,128)S(1)}, u32[]{:S(2)}, u32[]{:S(2)}) collective-permute-start(f32[264,256]{1,0:T(8,128)S(1)} %get-tuple-element.17), channel_id=1, source_target_pairs={{32,0},{40,8},{16,48},{24,56},{96,64},{104,72},{80,112},{88,120},{... | collective-permute-start | bytes 811016 | tf_op jit(solution)/shard_map/ppermute | solution.py:302
  123.8 3.4 %collective-permute-start.5 = (f32[264,256]{1,0:T(8,128)S(1)}, f32[264,256]{1,0:T(8,128)S(1)}, u32[]{:S(2)}, u32[]{:S(2)}) collective-permute-start(f32[264,256]{1,0:T(8,128)S(1)} %collective-permute-done.4.came_ref), channel_id=1, source_target_pairs={{0,8},{8,0},{16,24},{24,16},{32,40},{40,32},{48,56},{56,48},{64,72... | collective-permute-start | bytes 811016 | tf_op jit(solution)/shard_map/ppermute | solution.py:303
  127.9 0.7 collective-permute-start.6
  128.6 3.4 %collective-permute-start.7 = (f32[264,256]{1,0:T(8,128)S(1)}, f32[264,256]{1,0:T(8,128)S(1)}, u32[]{:S(2)}, u32[]{:S(2)}) collective-permute-start(f32[264,256]{1,0:T(8,128)S(1)} %collective-permute-done.6.came_ref), channel_id=1, source_target_pairs={{0,8},{8,0},{16,24},{24,16},{32,40},{40,32},{48,56},{56,48},{64,72... | collective-permute-start | bytes 811016 | tf_op jit(solution)/shard_map/ppermute | solution.py:303
  132.7 0.7 collective-permute-start.8
  133.4 3.4 %collective-permute-start.9 = (f32[264,256]{1,0:T(8,128)S(1)}, f32[264,256]{1,0:T(8,128)S(1)}, u32[]{:S(2)}, u32[]{:S(2)}) collective-permute-start(f32[264,256]{1,0:T(8,128)S(1)} %collective-permute-done.8.came_ref), channel_id=1, source_target_pairs={{0,8},{8,0},{16,24},{24,16},{32,40},{40,32},{48,56},{56,48},{64,72... | collective-permute-start | bytes 811016 | tf_op jit(solution)/shard_map/ppermute | solution.py:303
  137.4 0.7 collective-permute-start.10
  138.1 3.4 %collective-permute-start.11 = (f32[264,256]{1,0:T(8,128)S(1)}, f32[264,256]{1,0:T(8,128)S(1)}, u32[]{:S(2)}, u32[]{:S(2)}) collective-permute-start(f32[264,256]{1,0:T(8,128)S(1)} %collective-permute-done.10.came_ref), channel_id=1, source_target_pairs={{0,8},{8,0},{16,24},{24,16},{32,40},{40,32},{48,56},{56,48},{64,72... | collective-permute-start | bytes 811016 | tf_op jit(solution)/shard_map/ppermute | solution.py:303
  143.2 62.2 %collective-permute-start.12 = (f32[3,32,4]{2,1,0:T(8,128)S(1)}, f32[3,32,4]{2,1,0:T(8,128)S(1)}, u32[]{:S(2)}, u32[]{:S(2)}) collective-permute-start(f32[3,32,4]{2,1,0:T(8,128)S(1)} %constant_dynamic-slice_fusion), channel_id=1, source_target_pairs={{0,16},{8,24},{48,32},{56,40},{64,80},{72,88},{112,96},{120,104},{... | collective-permute-start | bytes 4616 | tf_op jit(solution)/shard_map/ppermute | solution.py:315
